TPU v7x, 256 devices: a whole 4x4x8 slice. The times are simulated.
256 devices in a mesh: row: 32 (over z, y), col: 8 (over x, core).
Axes of the slice: x: 4, y: 4, z: 8, core: 2. Of those that a mesh axis runs over, the one named last changes fastest.
Arguments:
- activations: bfloat16 [2048, 8192], P('col', 'row'), may hold values from -640 to 640
- output_grads: bfloat16 [2048, 24576], P('row', 'col'), may hold values from -640 to 640
- first_codes: int32 [8192, 12288], P('row', 'col'), may hold values from 0 to 255
- second_codes: int32 [8192, 12288], P('row', 'col'), may hold values from 0 to 255
- first_scales: float32 [8192, 192], P('row', 'col'), may hold values from 0.1 to 1
- second_rows: float32 [8192], P('row'), may hold values from 0.03 to 0.3
- second_cols: float32 [24576], P('col'), may hold values from 0.03 to 0.3
Outputs:
- update: float32 [8192, 24576], P('row', 'col')
- first_normed: bfloat16 [8192, 24576], P('row', 'col')
- first_peaks: float32 [8192, 192], P('row', 'col')
- second_normed: bfloat16 [8192, 24576], P('row', 'col')
- second_row_peaks: float32 [8192], P('row')
- second_col_peaks: float32 [24576], P('col')
All inputs are finite; a program needn't handle non-finite values. Where the computation divides by a largest or mean magnitude, that divisor is 1e-20 or more.
Results may differ from a plain program's by a relative error of at most 0.001.
Values may be sent and summed in bfloat16 or wider, within the bound.
A program may use at most 128 MiB of HBM per device.

v0:
```python
import jax
import jax.numpy as jnp
from jax import lax
from jax.sharding import PartitionSpec as P

D = 8192
FF = 24576


bias_one = 1.0 - 0.9**10
bias_two = 1.0 - 0.95**10


def decode(packed):
    height = packed.shape[0]
    low_half = jnp.bitwise_and(packed, 15).reshape(height, -1, 1, 128)
    high_half = jnp.right_shift(packed, 4).reshape(height, -1, 1, 128)
    return (
        jnp.concatenate([low_half, high_half], axis=2).reshape(height, -1, 128).astype(jnp.float32)
    )


def advance(
    gradient, clip_factor, first_codes, second_codes, first_scales, second_rows, second_cols
):
    height = gradient.shape[0]
    scaled = clip_factor * gradient.reshape(height, -1, 128)
    first_old = first_scales[:, :, None] * ((decode(first_codes) - 7.5) / 7.5)
    rank_scale = jnp.minimum(second_rows[:, None], second_cols[None, :]).reshape(height, -1, 128)
    second_old = rank_scale * ((decode(second_codes) + 1.0) / 16.0)
    new_first = 0.9 * first_old + 0.1 * scaled
    new_second = 0.95 * second_old + 0.05 * scaled * scaled
    update = new_first / bias_one / (jnp.sqrt(new_second / bias_two) + 1e-08)
    first_peaks = jnp.max(jnp.abs(new_first), axis=2)
    first_normed = (new_first / (first_peaks[:, :, None] + 1e-06)).astype(jnp.bfloat16)
    return (
        update.reshape(height, -1),
        first_normed.reshape(height, -1),
        first_peaks,
        new_second.reshape(height, -1),
    )


def local(
    activations, output_grads, first_codes, second_codes, first_scales, second_rows, second_cols
):
    gathered = lax.all_gather(activations, "col", axis=0, tiled=True)
    contract = (((0,), (0,)), ((), ()))
    grad_panels = lax.all_gather(output_grads, "row", axis=0, tiled=True)
    gradient = lax.dot_general(gathered, grad_panels, contract, preferred_element_type=jnp.float32)
    sumsq = lax.psum(jnp.sum(gradient * gradient), ("row", "col"))
    clip_factor = jnp.minimum(1.0, jnp.sqrt(jnp.float32(D * FF) / sumsq))
    update, first_normed, first_peaks, new_second = advance(
        gradient, clip_factor, first_codes, second_codes, first_scales, second_rows, second_cols
    )
    row_peaks = lax.pmax(jnp.max(new_second, axis=1), "col")
    col_peaks = lax.pmax(jnp.max(new_second, axis=0), "row")
    second_normed = (new_second / jnp.minimum(row_peaks[:, None], col_peaks[None, :])).astype(
        jnp.bfloat16
    )
    return (update, first_normed, first_peaks, second_normed, row_peaks, col_peaks)


def solution(mesh):
    return jax.shard_map(
        local,
        mesh=mesh,
        in_specs=(
            P("col", "row"),
            P("row", "col"),
            P("row", "col"),
            P("row", "col"),
            P("row", "col"),
            P("row"),
            P("col"),
        ),
        out_specs=(
            P("row", "col"),
            P("row", "col"),
            P("row", "col"),
            P("row", "col"),
            P("row"),
            P("col"),
        ),
        check_vma=False,
    )
```

profile of v0, /device:TPU:2, one launch (start us, length us, event | category | flops | bytes accessed | tf_op | source)
XLA Modules:
  0.0 439.5 jit_solution(9022976274627206167)
XLA Ops:
  7.2 0.0 all-gather.3.cloned.1.call-start
  7.2 0.7 all-gather.3.cloned.1.call-update
  7.9 0.0 all-gather.5.cloned.1.call-start
  7.9 0.7 all-gather.5.cloned.1.call-update
  8.6 0.7 broadcast_multiply_fusion
  9.4 0.1 copy.43
  9.5 1.9 copy.44
  11.4 0.2 broadcast_and_fusion
  11.6 0.6 fusion.6
  12.2 3.4 copy.46
  15.6 0.0 copy-start.5
  15.6 5.6 %div.47 = f32[256,3072]{1,0:T(8,128)} reshape(f32[256,12,2,128]{3,2,1,0:T(2,128)} %copy.46) | data formatting | bytes 6291456 | tf_op jit(solution)/shard_map/div | solution.py:30
  21.2 0.0 copy-done.5
  21.2 0.5 copy.40
  21.6 0.2 broadcast_and_fusion.1
  21.8 0.0 copy-start.3
  21.9 0.0 copy-start.4
  21.9 1.1 copy-done.3
  23.0 0.5 copy-done.4
  23.5 0.4 fusion.4
  23.9 3.4 copy.42
  27.3 4.1 sub.6
  31.4 0.0 copy-start.8
  31.4 0.0 copy-start.10
  31.4 5.6 %all-gather.3.cloned.1.call-done = bf16[2048,256]{1,0:T(8,128)(2,1)} async-done(((bf16[256,256]{1,0:T(8,128)(2,1)}), bf16[2048,256]{1,0:T(8,128)(2,1)}) %all-gather.3.cloned.1.call-update) | async-done | bytes 1048592 | tf_op jit(solution)/shard_map/all_gather | solution.py:47
  37.1 123.9 %all-gather.5.cloned.1.call-done = bf16[2048,3072]{1,0:T(8,128)(2,1)} async-done(((bf16[64,3072]{1,0:T(8,128)(2,1)}), bf16[2048,3072]{1,0:T(8,128)(2,1)}) %all-gather.5.cloned.1.call-update) | async-done | bytes 12582928 | tf_op jit(solution)/shard_map/all_gather | solution.py:49
  160.9 10.6 %multiply_reduce_fusion = (f32[]{:T(128)}, f32[256,3072]{1,0:T(8,128)}) fusion(bf16[2048,256]{1,0:T(8,128)(2,1)} %all-gather.3.cloned.1.call-done, bf16[2048,3072]{1,0:T(8,128)(2,1)} %all-gather.5.cloned.1.call-done), kind=kOutput, calls=%fused_computation.15 | convolution fusion | flops 3222798336 | bytes 16777220 | tf_op jit(solution)/shard_map/dot_general | solution.py:50
  171.6 73.9 %psum.7 = f32[]{:T(128)} all-reduce(f32[]{:T(128)} %get-tuple-element.16), channel_id=1, replica_groups=mesh['row'=32,'col'=8] {'row','col'}, use_global_device_ids=true, to_apply=%region_1.0 | all-reduce | flops 1 | bytes 8 | tf_op jit(solution)/shard_map/psum | solution.py:51
  246.2 0.0 copy-done.8
  246.2 0.0 copy-done.10
  246.2 5.5 %fusion.7 = (f32[256]{0:T(256)S(1)}, f32[3072]{0:T(1024)S(1)}, f32[256,3072]{1,0:T(8,128)}) fusion(f32[256,3072]{1,0:T(8,128)} %get-tuple-element.17, f32[]{:T(128)S(6)} %min.32, f32[256,3072]{1,0:T(8,128)} %div.47, f32[3072]{0:T(1024)S(1)} %copy-done.8, f32[256]{0:T(256)S(1)} %copy-done.10), kind=kLoop, calls=%fused_computation.23 | loop fusion | flops 7074560 | bytes 9463812 | tf_op jit(solution)/shard_map/reduce_max | solution.py:56
  251.8 139.4 %pmax.15 = f32[3072]{0:T(1024)S(1)} all-reduce(f32[3072]{0:T(1024)S(1)} %get-tuple-element.7), channel_id=1, replica_groups=mesh['row'=32,'col'=8] {'row'}, use_global_device_ids=true, to_apply=%region_6.0 | all-reduce | flops 3072 | bytes 24576 | tf_op jit(solution)/shard_map/pmax | solution.py:57
  391.2 0.0 copy-start.7
  391.2 11.1 %pmax.14 = f32[256]{0:T(256)S(1)} all-reduce(f32[256]{0:T(256)S(1)} %get-tuple-element.6), channel_id=1, replica_groups=mesh['row'=32,'col'=8] {'col'}, use_global_device_ids=true, to_apply=%region_4.0 | all-reduce | flops 256 | bytes 2048 | tf_op jit(solution)/shard_map/pmax | solution.py:56
  402.3 0.0 copy-start.9
  402.3 0.0 copy-start.2
  402.3 0.9 mul.90
  403.2 0.0 copy-start
  403.2 1.1 copy-done.2
  404.3 6.4 %add_divide_fusion = (f32[256,3072]{1,0:T(8,128)}, f32[256,3072]{1,0:T(8,128)}, bf16[256,3072]{1,0:T(8,128)(2,1)}) fusion(f32[256,3072]{1,0:T(8,128)} %get-tuple-element.8, f32[256,3072]{1,0:T(8,128)S(1)} %sub.6, f32[32,8,24,128]{3,2,1,0:T(8,128)S(1)} %bitcast.26, f32[256,3072]{1,0:T(8,128)S(1)} %copy-done.2, f32[]{:T(128)S(6)} %min.32, f32[3072]{0:T(1024)S(1)} %pmax.15, ...), kind=kLoop, calls=%fused_computation.14 | loop fusion | flops 9437184 | bytes 20460548 | tf_op jit(solution)/shard_map/div | solution.py:33
  410.7 0.0 copy-done.7
  410.7 0.0 copy-done.9
  410.7 0.0 copy-done
  410.7 5.6 %mul.111 = f32[256,12,2,128]{3,2,1,0:T(2,128)} reshape(f32[256,3072]{1,0:T(8,128)} %get-tuple-element.10) | data formatting | bytes 6291456 | tf_op jit(solution)/shard_map/mul | solution.py:31
  416.3 5.9 %copy.48 = f32[256,12,2,128]{0,3,1,2:T(8,128)} copy(f32[256,12,2,128]{3,2,1,0:T(2,128)} %mul.111) | data formatting | bytes 6291456 | tf_op jit(solution)/shard_map/mul | solution.py:31
  422.1 3.6 abs_reduce_fusion
  425.8 0.0 copy-start.6
  425.9 0.1 copy.50
  426.0 0.0 copy-start.1
  426.0 0.9 div.51
  426.8 1.0 copy-done.1
  427.9 4.8 %fusion.1 = bf16[256,3072]{1,0:T(8,128)(2,1)} fusion(f32[32,8,24,128]{3,2,1,0:T(8,128)S(1)} %bitcast.32, f32[256,3072]{1,0:T(8,128)} %get-tuple-element.10, f32[256,3072]{1,0:T(8,128)S(1)} %sub.6, f32[32,8,24,128]{3,2,1,0:T(8,128)S(1)} %bitcast.27), kind=kLoop, calls=%fused_computation.3 | loop fusion | flops 3932160 | bytes 14155776 | tf_op jit(solution)/shard_map/convert_element_type | solution.py:35
  432.7 0.0 copy-done.6
  (5 shorter events, 0.1 us)
Async XLA Ops:
  7.2 29.9 %all-gather.3.cloned.1.call-start = ((), (), s32[]{:S(2)}) async-start(), calls=%async_computation | async-start | bytes 1179648 | tf_op jit(solution)/shard_map/all_gather | solution.py:47
  7.9 153.0 %all-gather.5.cloned.1.call-start = ((), (), s32[]{:S(2)}) async-start(), calls=%async_computation.1 | async-start | bytes 12976128 | tf_op jit(solution)/shard_map/all_gather | solution.py:49
  15.6 5.6 %copy-start.5 = (s32[256,1536]{1,0:T(8,128)S(1)}, s32[256,1536]{1,0:T(8,128)}, u32[]{:S(2)}) copy-start(s32[256,1536]{1,0:T(8,128)} %param.9) | copy-start | bytes 4718596
  21.8 1.1 copy-start.3
  21.9 1.7 copy-start.4
  31.4 214.8 %copy-start.8 = (f32[3072]{0:T(1024)S(1)}, f32[3072]{0:T(1024)}, u32[]{:S(2)}) copy-start(f32[3072]{0:T(1024)} %param.13) | copy-start | bytes 36868
  31.4 214.8 %copy-start.10 = (f32[256]{0:T(256)S(1)}, f32[256]{0:T(256)}, u32[]{:S(2)}) copy-start(f32[256]{0:T(256)} %param.12) | copy-start | bytes 3076
  391.2 19.5 %copy-start.7 = (f32[3072]{0:T(1024)}, f32[3072]{0:T(1024)S(1)}, u32[]{:S(2)}) copy-start(f32[3072]{0:T(1024)S(1)} %pmax.15) | copy-start | bytes 36868
  402.3 8.4 %copy-start.9 = (f32[256]{0:T(256)}, f32[256]{0:T(256)S(1)}, u32[]{:S(2)}) copy-start(f32[256]{0:T(256)S(1)} %pmax.14) | copy-start | bytes 3076
  402.3 2.0 copy-start.2
  403.2 7.5 %copy-start = (f32[256,24,128]{2,1,0:T(8,128)}, f32[256,24,128]{2,1,0:T(8,128)S(1)}, u32[]{:S(2)}) copy-start(f32[256,24,128]{2,1,0:T(8,128)S(1)} %mul.90) | copy-start | bytes 9437188
  425.8 6.9 %copy-start.6 = (f32[256,24]{0,1:T(8,128)}, f32[256,24]{0,1:T(8,128)S(1)}, u32[]{:S(2)}) copy-start(f32[256,24]{0,1:T(8,128)S(1)} %reduce_max.30) | copy-start | bytes 73732
  426.0 1.9 copy-start.1
Sparse Core Ops, SparseCore 0:
  9.9 27.1 all-gather.2
  39.7 121.2 all-gather.4
where the time goes:
time: 444 us; the launch traced here: 440 us
  blocking collectives  224 us (50%)
  waiting for transfers between devices  131 us (30%)
  local copies, waits for them, and re-layouts  36.1 us (8%)
  other arithmetic  22.5 us (5%)
  between operations  15 us (3%)
  matrix products  10.6 us (2%)
    pmax x1, blocking collectives, local(): col_peaks = lax.pmax(jnp.max(new_second, axis=0), 'row')  139 us
    all_gather x1, waiting for transfers between devices, local(): grad_panels = lax.all_gather(output_grads, 'row', axis=0, tiled=True)  124 us
    psum x1, blocking collectives, local(): sumsq = lax.psum(jnp.sum(gradient * gradient), ('row', 'col'))  73.9 us
    mul x2, local copies, waits for them, and re-layouts, advance(): new_first = 0.9 * first_old + 0.1 * scaled  11.5 us
    pmax x1, blocking collectives, local(): row_peaks = lax.pmax(jnp.max(new_second, axis=1), 'col')  11.1 us
    dot_general x1, matrix products, local(): lax.dot_general(gathered, grad_panels, contract, preferred_element_type=j...  10.6 us
    div x2, local copies, waits for them, and re-layouts, advance(): second_old = rank_scale * ((decode(second_codes) + 1.0) / 16.0)  8.96 us
  transfers between devices with their start and end apart: 2, of which 2 were waited for; matrix products, arithmetic and copies ran while one was open for 5% of the time, Pallas kernels for 0%

commit v1 on v0

v1 whole, which is shorter than its diff:
```python
import functools

import jax
import jax.numpy as jnp
from jax import lax
from jax.experimental import pallas as pl
from jax.experimental.pallas import tpu as pltpu
from jax.sharding import PartitionSpec as P

MESH = pl.DeviceIdType.MESH
D = 8192
FF = 24576
TOKENS = 2048
ROWS = 256
COLS = 3072
NZ, NY, NX = 8, 4, 4
PART = COLS // NY
CHUNKS = 6
WIDTH = PART // CHUNKS
LANES = 128
WB = WIDTH // LANES
BLOCKS = COLS // LANES
ZROWS = TOKENS // NZ
TOK = TOKENS // (NZ * NY)

BIAS_ONE = 1.0 - 0.9**10
BIAS_TWO = 1.0 - 0.95**10


class Copies:
    def __init__(self, send, recv):
        self.send, self.recv = send, recv
        self.made = {}

    def start(self, key, src, dst, device):
        slot = len(self.made)
        copy = pltpu.make_async_remote_copy(
            src_ref=src,
            dst_ref=dst,
            send_sem=self.send.at[slot],
            recv_sem=self.recv.at[slot],
            device_id=device,
            device_id_type=MESH,
        )
        copy.start()
        self.made[key] = copy

    def arrived(self, key):
        self.made[key].wait_recv()

    def finish(self):
        for copy in self.made.values():
            copy.wait_send()


def n_copies():
    return CHUNKS * 3 + CHUNKS * 8 + 6 + 24 + 4 + CHUNKS * 3 + 14 + 10 + 4


def gather_kernel(
    act,
    grads,
    codes2_hbm,
    rows,
    cols,
    g_out,
    clip_out,
    rows_out,
    rinv_out,
    rp_out,
    cp_out,
    at,
    bb,
    gs,
    go,
    quad,
    codes2,
    sq,
    ss_src,
    ss_dst,
    cp_a,
    cp_b,
    cp_dst,
    rp_a,
    rp_b,
    rp_dst,
    rowacc,
    colacc,
    send,
    recv,
    local,
):
    r, c = lax.axis_index("row"), lax.axis_index("col")
    z, y = r // NY, r % NY
    x, k = c // 2, c % 2

    def to_z(d):
        return ((z + d + NZ) % NZ * NY + y, c)

    def to_y(d):
        return (z * NY + (y + d) % NY, c)

    def to_x(d):
        return (r, (x + d) % NX * 2 + k)

    peer = (r, x * 2 + 1 - k)

    load = pltpu.make_async_copy(codes2_hbm, codes2, local.at[0])
    load.start()

    barrier = pltpu.get_barrier_semaphore()
    partners = (
        [to_y(d) for d in (1, 3, 2)]
        + [to_x(d) for d in (1, 3, 2)]
        + [peer]
        + [to_z(d) for d in range(1, NZ)]
    )
    for partner in partners:
        pl.semaphore_signal(barrier, inc=1, device_id=partner, device_id_type=MESH)

    def spot(yy, cc, half=None):
        if half is None:
            return at.at[pl.ds(yy * ROWS, ROWS), pl.ds(cc * ROWS, ROWS)]
        size = ROWS // 2
        return at.at[pl.ds(yy * ROWS + half * size, size), pl.ds(cc * ROWS, ROWS)]

    spot(y, c)[...] = act[...].T

    def b_part(n, zz):
        return bb.at[n, pl.ds(zz * ZROWS, ZROWS)]

    owns = []
    for n in range(CHUNKS):
        own = pltpu.make_async_copy(
            grads.at[:, pl.ds(y * PART + n * WIDTH, WIDTH)],
            bb.at[n, pl.ds(z * ZROWS + y * TOK, TOK)],
            local.at[2 + n],
        )
        own.start()
        owns.append(own)
    pl.semaphore_wait(barrier, len(partners))

    net = Copies(send, recv)
    ring = (1, 3, 2)

    def spread(n):
        for d in ring:
            other = (y + d) % NY
            net.start(
                ("b1", n, d),
                grads.at[:, pl.ds(other * PART + n * WIDTH, WIDTH)],
                bb.at[n, pl.ds(z * ZROWS + y * TOK, TOK)],
                to_y(d),
            )

    def pass_on(n, s):
        if s == 1:
            owns[n].wait()
            for d in ring:
                net.arrived(("b1", n, d))
        for way in (1, -1):
            if s > 1:
                net.arrived(("b2", n, s - 1, way))
            zz = (z - way * (s - 1) + NZ) % NZ
            if s < 4:
                ref = b_part(n, zz)
            else:
                half = ZROWS // 2
                ref = bb.at[n, pl.ds(zz * ZROWS + (half if way < 0 else 0), half)]
            net.start(("b2", n, s, way), ref, ref, to_z(way))

    spread(0)
    for d in ring:
        ref = spot(y, c, 0)
        net.start(("ay", 0, d), ref, ref, to_y(d))
        ref = spot(y, c, 1)
        net.start(("ax", 0, d), ref, ref, to_x(d))
    for d in ring:
        ref = spot(y, c, 0)
        net.start(("axy", 0, d), ref, ref, to_x(d))
    spread(1)
    for d in ring:
        ref = spot(y, c, 1)
        net.start(("ayx", 0, d), ref, ref, to_y(d))
    for n in range(2, CHUNKS):
        spread(n)
    pass_on(0, 1)
    for e in ring:
        net.arrived(("ay", 0, e))
        ref = spot((y + NY - e) % NY, c, 0)
        for d in ring:
            net.start(("axy", e, d), ref, ref, to_x(d))
        net.arrived(("ax", 0, e))
        ref = spot(y, (x + NX - e) % NX * 2 + k, 1)
        for d in ring:
            net.start(("ayx", e, d), ref, ref, to_y(d))

    def to_peer(q):
        if q == 0:
            for d in ring:
                net.arrived(("ayx", 0, d))
        else:
            for e in (0,) + ring:
                net.arrived(("axy", e, q))
            for d in ring:
                net.arrived(("ayx", q, d))
        ref = at.at[:, pl.ds(((x + NX - q) % NX * 2 + k) * ROWS, ROWS)]
        net.start(("peer", q), ref, ref, peer)

    def decode_second():
        load.wait()
        spread_rows = jnp.broadcast_to(rows[...].reshape(1, ROWS), (LANES, ROWS)).T
        rows_out[...] = spread_rows

        def body(i, carry):
            at_rows = pl.ds(pl.multiple_of(i * 32, 32), 32)
            row = rows_out[at_rows, :] * (0.95 / 16.0)
            for w in range(BLOCKS // 2):
                word = codes2[at_rows, pl.ds(w * LANES, LANES)]
                for h in range(2):
                    b = 2 * w + h
                    code = word & 15 if h == 0 else word >> 4
                    col = cols[pl.ds(b * LANES, LANES)].reshape(1, LANES) * (0.95 / 16.0)
                    quad[b, at_rows, :] = jnp.minimum(row, col) * (code.astype(jnp.float32) + 1.0)
            return carry

        lax.fori_loop(0, ROWS // 32, body, 0)

    sq[...] = jnp.zeros_like(sq)

    def multiply(n):
        for d in (2, 1, 3, 0):
            other = (y + d) % NY
            res = jnp.dot(
                at[pl.ds(pl.multiple_of(other * ROWS, ROWS), ROWS), :],
                bb[n],
                preferred_element_type=jnp.float32,
            )
            sq[...] += jnp.sum((res * res).reshape(ROWS // 8, 8, WIDTH), axis=0)
            place = pl.ds(y * (PART // LANES) + n * WB, WB)
            for w in range(WB):
                piece = res[:, w * LANES : (w + 1) * LANES]
                if d:
                    gs[n, d - 1, w] = piece
                else:
                    go[y * (PART // LANES) + n * WB + w] = piece
            if d:
                net.start(("out", n, d), gs.at[n, d - 1], go.at[place], to_y(d))

    extra = {
        2: [decode_second],
        4: [lambda: to_peer(0)],
        5: [lambda: to_peer(1), lambda: to_peer(3), lambda: to_peer(2)],
    }
    done = 0
    for slot in range(2, CHUNKS + 5):
        for n in range(CHUNKS):
            s = slot - n
            if 1 <= s <= 4 and (n, s) != (0, 1):
                pass_on(n, s)
        for step in extra.get(slot, ()):
            step()
        if slot >= 6 or slot == CHUNKS + 4:
            last = slot == CHUNKS + 4
            upto = CHUNKS if last else slot - 5
            if done == 0:
                for q in (0,) + ring:
                    net.arrived(("peer", q))
            while done < upto:
                for way in (1, -1):
                    net.arrived(("b2", done, 4, way))
                multiply(done)
                done += 1

    ss_src[0] = jnp.full((8, LANES), jnp.sum(sq[...]))
    slot = 0
    stages = [
        [("ss", 0, 0, peer)],
        [("ss", 1, d, to_x(d)) for d in ring],
        [("ss", 2, d, to_y(d)) for d in ring],
        [("ss", 3, d, to_z(d)) for d in range(1, NZ)],
    ]
    for i, stage in enumerate(stages):
        for j, (name, _, d, device) in enumerate(stage):
            net.start((name, i, d), ss_src.at[i], ss_dst.at[slot + j], device)
        total = ss_src[i]
        for j, (name, _, d, device) in enumerate(stage):
            net.arrived((name, i, d))
            total = total + ss_dst[slot + j]
        slot += len(stage)
        if i < 3:
            ss_src[i + 1] = total
    limit = float(D) * FF
    clip = jnp.where(total <= limit, 1.0, jnp.sqrt(limit / jnp.maximum(total, limit)))
    clip_out[...] = clip

    for n in range(CHUNKS):
        for d in ring:
            net.arrived(("out", n, d))
    save = pltpu.make_async_copy(go, g_out, local.at[1])
    save.start()

    rate = clip[0:1, :]
    colacc[...] = jnp.zeros_like(colacc)

    def body(i, carry):
        at_rows = pl.ds(pl.multiple_of(i * 32, 32), 32)
        best = jnp.zeros((32, LANES), jnp.float32)
        for b in range(BLOCKS):
            scaled = rate * go[b, at_rows, :]
            second = quad[b, at_rows, :] + 0.05 * scaled * scaled
            best = jnp.maximum(best, second)
            colacc[b] = jnp.maximum(colacc[b], jnp.max(second.reshape(4, 8, LANES), axis=0))
        rowacc[at_rows, :] = best
        return carry

    lax.fori_loop(0, ROWS // 32, body, 0)
    rp_a[...] = jnp.broadcast_to(
        jnp.max(rowacc[...].T, axis=0, keepdims=True), (8, ROWS)
    )
    for b in range(BLOCKS):
        cp_a[b : b + 1, :] = jnp.max(colacc[b], axis=0, keepdims=True)

    for j, d in enumerate(ring):
        net.start(("cy", d), cp_a, cp_dst.at[j], to_y(d))
    net.start(("rk",), rp_a, rp_dst.at[0], peer)
    net.arrived(("rk",))
    rp_b[...] = jnp.maximum(rp_a[...], rp_dst[0])
    for j, d in enumerate(ring):
        net.start(("rx", d), rp_b, rp_dst.at[1 + j], to_x(d))
    for d in ring:
        net.arrived(("cy", d))
    cp_b[...] = jnp.maximum(
        jnp.maximum(cp_a[...], cp_dst[0]), jnp.maximum(cp_dst[1], cp_dst[2])
    )
    for d in range(1, NZ):
        net.start(("cz", d), cp_b, cp_dst.at[2 + d], to_z(d))
    peaks = rp_b[...]
    for j, d in enumerate(ring):
        net.arrived(("rx", d))
        peaks = jnp.maximum(peaks, rp_dst[1 + j])
    rp_out[...] = peaks
    rinv_out[...] = jnp.broadcast_to((1.0 / peaks)[0:1, :], (LANES, ROWS)).T
    tops = cp_b[...]
    for d in range(1, NZ):
        net.arrived(("cz", d))
        tops = jnp.maximum(tops, cp_dst[2 + d])
    cp_out[...] = tops
    save.wait()
    net.finish()


def adam_kernel(
    g,
    clip,
    codes1,
    codes2,
    scales,
    row_scale,
    cols,
    row_inv,
    rp,
    cp,
    update,
    first_normed,
    first_peaks,
    second_normed,
    row_peaks,
    col_peaks,
    cinv,
):
    @pl.when(pl.program_id(0) == 0)
    def _():
        row_peaks[...] = rp[0:1, :].reshape(ROWS)
        for b in range(BLOCKS):
            col_peaks[pl.ds(b * LANES, LANES)] = cp[b : b + 1, :].reshape(LANES)
        cinv[...] = 1.0 / cp[...]

    height = codes1.shape[0]
    rate = clip[0:1, :]
    lane = lax.broadcasted_iota(jnp.int32, (height, LANES), 1)
    row = row_scale[...] * (0.95 / 16.0)
    rinv = row_inv[...]
    peaks = jnp.zeros((height, LANES), jnp.float32)
    for b in range(BLOCKS):
        at_word = pl.ds(b // 2 * LANES, LANES)
        at_cols = pl.ds(b * LANES, LANES)

        def code(ref):
            word = ref[:, at_word]
            return (word & 15 if b % 2 == 0 else word >> 4).astype(jnp.float32)

        scaled = rate * g[b]
        first = (scales[:, b : b + 1] * (0.9 / 7.5)) * (code(codes1) - 7.5) + 0.1 * scaled
        col = cols[at_cols].reshape(1, LANES) * (0.95 / 16.0)
        second = jnp.minimum(row, col) * (code(codes2) + 1.0) + 0.05 * scaled * scaled
        peak = jnp.max(jnp.abs(first), axis=1, keepdims=True)
        peaks = jnp.where(lane == b, peak, peaks)
        first_normed[:, at_cols] = (first * (1.0 / (peak + 1e-06))).astype(jnp.bfloat16)
        under = second * (1.0 / BIAS_TWO)
        root = under * lax.rsqrt(under)
        update[:, at_cols] = (first * (1.0 / BIAS_ONE)) / (root + 1e-08)
        second_normed[:, at_cols] = (second * jnp.maximum(rinv, cinv[b : b + 1, :])).astype(
            jnp.bfloat16
        )
    first_peaks[...] = peaks[:, :BLOCKS]


def local(activations, output_grads, first_codes, second_codes, first_scales, second_rows, second_cols):
    f32, bf16 = jnp.float32, jnp.bfloat16
    vmem = pl.BlockSpec(memory_space=pltpu.VMEM)
    hbm = pl.BlockSpec(memory_space=pl.ANY)
    g, clip, row_scale, row_inv, rp, cp = pl.pallas_call(
        gather_kernel,
        out_shape=(
            jax.ShapeDtypeStruct((BLOCKS, ROWS, LANES), f32),
            jax.ShapeDtypeStruct((8, LANES), f32),
            jax.ShapeDtypeStruct((ROWS, LANES), f32),
            jax.ShapeDtypeStruct((ROWS, LANES), f32),
            jax.ShapeDtypeStruct((8, ROWS), f32),
            jax.ShapeDtypeStruct((BLOCKS, LANES), f32),
        ),
        in_specs=[vmem, vmem, hbm, vmem, vmem],
        out_specs=(hbm, vmem, vmem, vmem, vmem, vmem),
        scratch_shapes=[
            pltpu.VMEM((NY * ROWS, TOKENS), bf16),
            pltpu.VMEM((CHUNKS, TOKENS, WIDTH), bf16),
            pltpu.VMEM((CHUNKS, 3, WB, ROWS, LANES), f32),
            pltpu.VMEM((BLOCKS, ROWS, LANES), f32),
            pltpu.VMEM((BLOCKS, ROWS, LANES), f32),
            pltpu.VMEM((ROWS, COLS // 2), jnp.int32),
            pltpu.VMEM((8, WIDTH), f32),
            pltpu.VMEM((4, 8, LANES), f32),
            pltpu.VMEM((14, 8, LANES), f32),
            pltpu.VMEM((BLOCKS, LANES), f32),
            pltpu.VMEM((BLOCKS, LANES), f32),
            pltpu.VMEM((10, BLOCKS, LANES), f32),
            pltpu.VMEM((8, ROWS), f32),
            pltpu.VMEM((8, ROWS), f32),
            pltpu.VMEM((4, 8, ROWS), f32),
            pltpu.VMEM((ROWS, LANES), f32),
            pltpu.VMEM((BLOCKS, 8, LANES), f32),
            pltpu.SemaphoreType.DMA((n_copies(),)),
            pltpu.SemaphoreType.DMA((n_copies(),)),
            pltpu.SemaphoreType.DMA((2 + CHUNKS,)),
        ],
        compiler_params=pltpu.CompilerParams(
            collective_id=0, has_side_effects=True, vmem_limit_bytes=48 * 2**20
        ),
        name="gather",
    )(activations, output_grads, second_codes, second_rows, second_cols)

    tile = 32

    def by_rows(*shape):
        return pl.BlockSpec(shape, lambda i: (i, 0))

    def whole(*shape):
        return pl.BlockSpec(shape, lambda i: (0,) * len(shape))

    return pl.pallas_call(
        adam_kernel,
        grid=(ROWS // tile,),
        out_shape=(
            jax.ShapeDtypeStruct((ROWS, COLS), f32),
            jax.ShapeDtypeStruct((ROWS, COLS), bf16),
            jax.ShapeDtypeStruct((ROWS, BLOCKS), f32),
            jax.ShapeDtypeStruct((ROWS, COLS), bf16),
            jax.ShapeDtypeStruct((ROWS,), f32),
            jax.ShapeDtypeStruct((COLS,), f32),
        ),
        in_specs=[
            pl.BlockSpec((BLOCKS, tile, LANES), lambda i: (0, i, 0)),
            whole(8, LANES),
            by_rows(tile, COLS // 2),
            by_rows(tile, COLS // 2),
            by_rows(tile, BLOCKS),
            by_rows(tile, LANES),
            whole(COLS),
            by_rows(tile, LANES),
            whole(8, ROWS),
            whole(BLOCKS, LANES),
        ],
        out_specs=(
            by_rows(tile, COLS),
            by_rows(tile, COLS),
            by_rows(tile, BLOCKS),
            by_rows(tile, COLS),
            whole(ROWS),
            whole(COLS),
        ),
        scratch_shapes=[pltpu.VMEM((BLOCKS, LANES), f32)],
        compiler_params=pltpu.CompilerParams(vmem_limit_bytes=32 * 2**20),
        name="adam",
    )(g, clip, first_codes, second_codes, first_scales, row_scale, second_cols, row_inv, rp, cp)


def solution(mesh):
    return jax.shard_map(
        local,
        mesh=mesh,
        in_specs=(
            P("col", "row"),
            P("row", "col"),
            P("row", "col"),
            P("row", "col"),
            P("row", "col"),
            P("row"),
            P("col"),
        ),
        out_specs=(
            P("row", "col"),
            P("row", "col"),
            P("row", "col"),
            P("row", "col"),
            P("row"),
            P("col"),
        ),
        check_vma=False,
    )
```

time: 444 us -> 115 us (0.26)
  blocking collectives: 224 us -> 0 us
  waiting for transfers between devices: 131 us -> 0 us
  Pallas kernels: 0 us -> 108 us
  local copies, waits for them, and re-layouts: 36.1 us -> 6.21 us
  other arithmetic: 22.5 us -> 0 us
  between operations: 15 us -> 0.66 us
  matrix products: 10.6 us -> 0 us
    pmax x2 -> x0, blocking collectives: 151 us -> none  [the longest x1 139 us: local(): col_peaks = lax.pmax(jnp.max(new_second, axis=0), 'row')]
    all_gather x2 -> x0, waiting for transfers between devices: 130 us -> none  [the longest x1 124 us: local(): grad_panels = lax.all_gather(output_grads, 'row', axis=0, tiled=True)]
    pallas_call x0 -> x2, Pallas kernels: none -> 108 us  [the longest x1 91.3 us: local(): pl.pallas_call(gather_kernel, out_shape=(jax.ShapeDtypeStruct((BLOCKS, RO...]
    psum x1 -> x0, blocking collectives: 73.9 us -> none  [local(): sumsq = lax.psum(jnp.sum(gradient * gradient), ('row', 'col'))]
    mul x6 -> x0, local copies, waits for them, and re-layouts: 12.5 us -> none  [the longest x2 11.5 us: advance(): new_first = 0.9 * first_old + 0.1 * scaled]
    dot_general x1 -> x0, matrix products: 10.6 us -> none  [local(): lax.dot_general(gathered, grad_panels, contract, preferred_element_type=j...]
    div x3 -> x0, local copies, waits for them, and re-layouts: 9.83 us -> none  [the longest x2 8.96 us: advance(): second_old = rank_scale * ((decode(second_codes) + 1.0) / 16.0)]
    reduce_max x2 -> x0, other arithmetic: 9.15 us -> none  [the longest x1 5.52 us: local(): row_peaks = lax.pmax(jnp.max(new_second, axis=1), 'col')]
  transfers between devices with their start and end apart: 2 -> 0, of which waited for: 2 -> 0; matrix products, arithmetic and copies ran while one was open for 5% -> 0% of each run, Pallas kernels for 0% -> 0%
where the time goes in v1:
time: 115 us
  Pallas kernels  108 us (94%)
  local copies, waits for them, and re-layouts  6.21 us (5%)
    pallas_call x1, Pallas kernels, local(): pl.pallas_call(gather_kernel, out_shape=(jax.ShapeDtypeStruct((BLOCKS, RO...  91.3 us
    pallas_call x1, Pallas kernels, local(): pl.pallas_call(adam_kernel, grid=(ROWS // tile,), out_shape=(jax.ShapeDty...  16.3 us
    unnamed x13, local copies, waits for them, and re-layouts  5.53 us

profile of v1, /device:TPU:2, one launch (start us, length us, event | category | flops | bytes accessed | tf_op | source)
XLA Modules:
  0.0 114.5 jit_solution(17166892534273823890)
XLA Ops:
  0.6 0.8 copy.13.scales
  1.5 0.0 copy-start
  1.5 1.4 %copy-done = s32[256,1536]{1,0:T(8,128)S(1)} copy-done((s32[256,1536]{1,0:T(8,128)S(1)}, s32[256,1536]{1,0:T(8,128)}, u32[]{:S(2)}) %copy-start) | copy-done | bytes 1572888
  2.9 0.0 copy-start.2
  2.9 1.0 copy-done.2
  3.9 0.0 copy-start.3
  3.9 0.9 copy-done.3
  4.8 0.0 copy-start.4
  4.8 0.7 copy-done.4
  5.5 0.0 copy-start.5
  5.5 0.7 copy-done.5
  6.2 0.0 copy-start.1
  6.2 91.3 %gather.1 = (f32[24,256,128]{2,1,0:T(8,128)S(1)}, f32[8,128]{1,0:T(8,128)S(1)}, f32[256,128]{1,0:T(8,128)S(1)}, f32[256,128]{1,0:T(8,128)S(1)}, f32[8,256]{1,0:T(8,128)S(1)}, /*index=5*/f32[24,128]{1,0:T(8,128)S(1)}) custom-call(bf16[256,256]{1,0:T(8,128)(2,1)S(1)} %copy-done.3, bf16[64,3072]{1,0:T(8,128)(2,1)S(1)} %copy-done.2, s32[256,1536]{1,0:T(8,128)S(1)} %copy-done, ...), custom_call_target="tpu_custom_call" | custom-call | tf_op jit(solution)/shard_map/gather/pallas_call | solution.py:413
  97.5 0.0 copy-done.1
  97.5 16.3 %adam.1 = (f32[256,3072]{1,0:T(8,128)}, bf16[256,3072]{1,0:T(8,128)(2,1)}, f32[256,24]{1,0:T(8,128)S(1)}, bf16[256,3072]{1,0:T(8,128)(2,1)}, f32[256]{0:T(256)}, /*index=5*/f32[3072]{0:T(1024)}) custom-call(f32[24,256,128]{2,1,0:T(8,128)S(1)} %get-tuple-element.12.g, f32[8,128]{1,0:T(8,128)S(1)} %get-tuple-element.13.clip, s32[256,1536]{1,0:T(8,128)S(1)} %copy-done.1, ...), custom_call_target="tpu_custom_call" | custom-call | tf_op jit(solution)/shard_map/adam/pallas_call | solution.py:461
  113.8 0.7 copy.14
Async XLA Ops:
  1.5 1.4 %copy-start = (s32[256,1536]{1,0:T(8,128)S(1)}, s32[256,1536]{1,0:T(8,128)}, u32[]{:S(2)}) copy-start(s32[256,1536]{1,0:T(8,128)} %codes2.1) | copy-start | bytes 4718596
  2.9 1.0 copy-start.2
  3.9 0.9 copy-start.3
  4.8 0.7 copy-start.4
  5.5 0.7 copy-start.5
  6.2 91.3 %copy-start.1 = (s32[256,1536]{1,0:T(8,128)S(1)}, s32[256,1536]{1,0:T(8,128)}, u32[]{:S(2)}) copy-start(s32[256,1536]{1,0:T(8,128)} %codes1.1) | copy-start | bytes 4718596

commit v2 on v1

v2 whole, which is shorter than its diff:
```python
import jax
import jax.numpy as jnp
from jax import lax
from jax.experimental import pallas as pl
from jax.experimental.pallas import tpu as pltpu
from jax.sharding import PartitionSpec as P

MESH = pl.DeviceIdType.MESH
D = 8192
FF = 24576
TOKENS = 2048
ROWS = 256
COLS = 3072
NZ, NY, NX = 8, 4, 4
PART = COLS // NY
CHUNKS = 6
WIDTH = PART // CHUNKS
LANES = 128
TILE = 32
FINISH = 64
BLOCKS = COLS // LANES
ZROWS = TOKENS // NZ
TOK = TOKENS // (NZ * NY)

BIAS_ONE = 1.0 - 0.9**10
BIAS_TWO = 1.0 - 0.95**10


class Copies:
    def __init__(self, send, recv):
        self.send, self.recv = send, recv
        self.made = {}

    def start(self, key, src, dst, device):
        slot = len(self.made)
        copy = pltpu.make_async_remote_copy(
            src_ref=src,
            dst_ref=dst,
            send_sem=self.send.at[slot],
            recv_sem=self.recv.at[slot],
            device_id=device,
            device_id_type=MESH,
        )
        copy.start()
        self.made[key] = copy

    def arrived(self, key):
        self.made[key].wait_recv()

    def finish(self):
        for copy in self.made.values():
            copy.wait_send()


def n_copies():
    return CHUNKS * (3 + 8 + 3 + 3) + 6 + 24 + 4 + 14 + 10 + 4


def step_kernel(
    act_hbm,
    grads,
    codes1_hbm,
    codes2_hbm,
    scales_hbm,
    rows_hbm,
    cols_hbm,
    update,
    first_normed,
    first_peaks,
    second,
    rinv_out,
    rp_out,
    cp_out,
    act,
    codes1,
    codes2,
    scales,
    rows,
    cols,
    at,
    bb,
    gs,
    gs_scale,
    gi,
    gi_scale,
    mom,
    sq,
    ss_src,
    ss_dst,
    cp_a,
    cp_b,
    cp_dst,
    rp_a,
    rp_b,
    rp_dst,
    rowacc,
    colacc,
    send,
    recv,
    local,
):
    r, c = lax.axis_index("row"), lax.axis_index("col")
    z, y = r // NY, r % NY
    x, k = c // 2, c % 2

    def to_z(d):
        return ((z + d + NZ) % NZ * NY + y, c)

    def to_y(d):
        return (z * NY + (y + d) % NY, c)

    def to_x(d):
        return (r, (x + d) % NX * 2 + k)

    peer = (r, x * 2 + 1 - k)

    barrier = pltpu.get_barrier_semaphore()
    partners = (
        [to_z(d) for d in range(1, NZ)]
        + [to_y(d) for d in (1, 3, 2)]
        + [to_x(d) for d in (1, 3, 2)]
        + [peer]
    )
    for partner in partners:
        pl.semaphore_signal(barrier, inc=1, device_id=partner, device_id_type=MESH)

    pairs = (
        (act_hbm, act),
        (codes2_hbm, codes2),
        (rows_hbm, rows),
        (cols_hbm, cols),
        (scales_hbm, scales),
        (codes1_hbm, codes1),
    )
    loads = [pltpu.make_async_copy(src, dst, local.at[i]) for i, (src, dst) in enumerate(pairs)]
    for load in loads:
        load.start()

    def spot(yy, cc, half=None):
        if half is None:
            return at.at[pl.ds(yy * ROWS, ROWS), pl.ds(cc * ROWS, ROWS)]
        size = ROWS // 2
        return at.at[pl.ds(yy * ROWS + half * size, size), pl.ds(cc * ROWS, ROWS)]

    def b_part(n, zz):
        return bb.at[n, pl.ds(zz * ZROWS, ZROWS)]

    owns = []
    for n in range(CHUNKS):
        own = pltpu.make_async_copy(
            grads.at[:, pl.ds(y * PART + n * WIDTH, WIDTH)],
            bb.at[n, pl.ds(z * ZROWS + y * TOK, TOK)],
            local.at[len(pairs) + n],
        )
        own.start()
        owns.append(own)
    loads[0].wait()
    spot(y, c)[...] = act[...].T

    def decode_second():
        for load in loads[1:4]:
            load.wait()
        rowacc[...] = jnp.broadcast_to(rows[...].reshape(1, ROWS), (LANES, ROWS)).T * (0.95 / 16.0)

        @pl.loop(0, ROWS // TILE)
        def _(i):
            at_rows = pl.ds(pl.multiple_of(i * TILE, TILE), TILE)
            row = rowacc[at_rows, :]
            for b in range(BLOCKS):
                word = codes2[at_rows, pl.ds(b // 2 * LANES, LANES)]
                code = word & 15 if b % 2 == 0 else word >> 4
                col = cols[pl.ds(b * LANES, LANES)].reshape(1, LANES) * (0.95 / 16.0)
                second[b, at_rows, :] = jnp.minimum(row, col) * (code.astype(jnp.float32) + 1.0)

    def decode_first():
        for load in loads[4:]:
            load.wait()
        wide = jnp.concatenate(
            [scales[...], jnp.zeros((LANES - BLOCKS, ROWS), jnp.float32)], axis=0
        )
        rowacc[...] = wide.T * (0.9 / 7.5)

        @pl.loop(0, ROWS // TILE)
        def _(i):
            at_rows = pl.ds(pl.multiple_of(i * TILE, TILE), TILE)
            scale = rowacc[at_rows, :]
            for b in range(BLOCKS):
                word = codes1[at_rows, pl.ds(b // 2 * LANES, LANES)]
                code = word & 15 if b % 2 == 0 else word >> 4
                mom[b, at_rows, :] = scale[:, b : b + 1] * (code.astype(jnp.float32) - 7.5)

    decode_second()
    pl.semaphore_wait(barrier, len(partners))

    net = Copies(send, recv)
    ring = (1, 3, 2)

    def spread(n):
        for d in ring:
            other = (y + d) % NY
            net.start(
                ("b1", n, d),
                grads.at[:, pl.ds(other * PART + n * WIDTH, WIDTH)],
                bb.at[n, pl.ds(z * ZROWS + y * TOK, TOK)],
                to_y(d),
            )

    def pass_on(n, s):
        if s == 1:
            owns[n].wait()
            for d in ring:
                net.arrived(("b1", n, d))
        for way in (1, -1):
            if s > 1:
                net.arrived(("b2", n, s - 1, way))
            zz = (z - way * (s - 1) + NZ) % NZ
            if s < 4:
                ref = b_part(n, zz)
            else:
                half = ZROWS // 2
                ref = bb.at[n, pl.ds(zz * ZROWS + (half if way < 0 else 0), half)]
            net.start(("b2", n, s, way), ref, ref, to_z(way))

    spread(0)
    for d in ring:
        ref = spot(y, c, 0)
        net.start(("ay", 0, d), ref, ref, to_y(d))
        ref = spot(y, c, 1)
        net.start(("ax", 0, d), ref, ref, to_x(d))
    for d in ring:
        ref = spot(y, c, 0)
        net.start(("axy", 0, d), ref, ref, to_x(d))
    spread(1)
    for d in ring:
        ref = spot(y, c, 1)
        net.start(("ayx", 0, d), ref, ref, to_y(d))
    for n in range(2, CHUNKS):
        spread(n)
    decode_first()
    pass_on(0, 1)
    for e in ring:
        net.arrived(("ay", 0, e))
        ref = spot((y + NY - e) % NY, c, 0)
        for d in ring:
            net.start(("axy", e, d), ref, ref, to_x(d))
        net.arrived(("ax", 0, e))
        ref = spot(y, (x + NX - e) % NX * 2 + k, 1)
        for d in ring:
            net.start(("ayx", e, d), ref, ref, to_y(d))

    def to_peer(q):
        if q == 0:
            for d in ring:
                net.arrived(("ayx", 0, d))
        else:
            for e in (0,) + ring:
                net.arrived(("axy", e, q))
            for d in ring:
                net.arrived(("ayx", q, d))
        ref = at.at[:, pl.ds(((x + NX - q) % NX * 2 + k) * ROWS, ROWS)]
        net.start(("peer", q), ref, ref, peer)

    sq[...] = jnp.zeros_like(sq)

    def multiply(n):
        for d in (2, 1, 3, 0):
            other = (y + d) % NY
            res = jnp.dot(
                at[pl.ds(pl.multiple_of(other * ROWS, ROWS), ROWS), :],
                bb[n],
                preferred_element_type=jnp.float32,
            )
            tiles = res.reshape(ROWS // 8, 8, WIDTH)
            sq[...] += jnp.sum(tiles * tiles, axis=0)
            top = jnp.max(jnp.max(jnp.abs(tiles), axis=0), axis=0, keepdims=True)
            top = jnp.maximum(top, 1e-30)
            words = jnp.round(res * (32767.0 / top)).astype(jnp.int32).astype(jnp.int16)
            scale = jnp.broadcast_to(top * (1.0 / 32767.0), (8, LANES))
            block = y * (PART // LANES) + n
            if d:
                gs[n, d - 1] = words
                gs_scale[n, d - 1] = scale
                net.start(("out", n, d), gs.at[n, d - 1], gi.at[block], to_y(d))
                net.start(("scale", n, d), gs_scale.at[n, d - 1], gi_scale.at[block], to_y(d))
            else:
                gi[block] = words
                gi_scale[block] = scale

    extra = {
        4: [lambda: to_peer(0)],
        5: [lambda: to_peer(1), lambda: to_peer(3), lambda: to_peer(2)],
    }
    done = 0
    for slot in range(2, CHUNKS + 5):
        for n in range(CHUNKS):
            s = slot - n
            if 1 <= s <= 4 and (n, s) != (0, 1):
                pass_on(n, s)
        for step in extra.get(slot, ()):
            step()
        if slot >= 6 or slot == CHUNKS + 4:
            last = slot == CHUNKS + 4
            upto = CHUNKS if last else slot - 5
            if done == 0:
                for q in (0,) + ring:
                    net.arrived(("peer", q))
            while done < upto:
                for way in (1, -1):
                    net.arrived(("b2", done, 4, way))
                multiply(done)
                done += 1

    ss_src[0] = jnp.full((8, LANES), jnp.sum(sq[...]))
    slot = 0
    stages = [
        [(0, peer)],
        [(d, to_x(d)) for d in ring],
        [(d, to_y(d)) for d in ring],
        [(d, to_z(d)) for d in range(1, NZ)],
    ]
    for i, stage in enumerate(stages):
        for j, (d, device) in enumerate(stage):
            net.start(("ss", i, d), ss_src.at[i], ss_dst.at[slot + j], device)
        total = ss_src[i]
        for j, (d, device) in enumerate(stage):
            net.arrived(("ss", i, d))
            total = total + ss_dst[slot + j]
        slot += len(stage)
        if i < 3:
            ss_src[i + 1] = total
    limit = float(D) * FF
    clip = jnp.where(total <= limit, 1.0, jnp.sqrt(limit / jnp.maximum(total, limit)))

    for n in range(CHUNKS):
        for d in ring:
            net.arrived(("out", n, d))
            net.arrived(("scale", n, d))

    rate = clip[0:1, :]
    colacc[...] = jnp.zeros_like(colacc)

    @pl.loop(0, ROWS // TILE)
    def _(i):
        at_rows = pl.ds(pl.multiple_of(i * TILE, TILE), TILE)
        best = jnp.zeros((TILE, LANES), jnp.float32)
        for b in range(BLOCKS):
            words = gi[b, at_rows, :].astype(jnp.int32).astype(jnp.float32)
            scaled = words * (gi_scale[b, 0:1, :] * rate)
            value = second[b, at_rows, :] + 0.05 * scaled * scaled
            second[b, at_rows, :] = value
            mom[b, at_rows, :] += 0.1 * scaled
            best = jnp.maximum(best, value)
            colacc[b] = jnp.maximum(colacc[b], jnp.max(value.reshape(TILE // 8, 8, LANES), axis=0))
        rowacc[at_rows, :] = best

    for b in range(BLOCKS):
        cp_a[b : b + 1, :] = jnp.max(colacc[b], axis=0, keepdims=True)
    for j, d in enumerate(ring):
        net.start(("cy", d), cp_a, cp_dst.at[j], to_y(d))
    rp_a[...] = jnp.broadcast_to(jnp.max(rowacc[...].T, axis=0, keepdims=True), (8, ROWS))
    net.start(("rk",), rp_a, rp_dst.at[0], peer)

    def advance(first, last):
        lane = lax.broadcasted_iota(jnp.int32, (TILE, LANES), 1)

        @pl.loop(first, last)
        def _(i):
            at_rows = pl.ds(pl.multiple_of(i * TILE, TILE), TILE)
            peaks = jnp.zeros((TILE, LANES), jnp.float32)
            for b in range(BLOCKS):
                at_cols = pl.ds(b * LANES, LANES)
                value = mom[b, at_rows, :]
                peak = jnp.max(jnp.abs(value), axis=1, keepdims=True)
                peaks = jnp.where(lane == b, peak, peaks)
                first_normed[at_rows, at_cols] = (value * inverse(peak + 1e-06)).astype(
                    jnp.bfloat16
                )
                under = second[b, at_rows, :] * (1.0 / BIAS_TWO)
                root = under * lax.rsqrt(under) + 1e-08
                update[at_rows, at_cols] = (value * (1.0 / BIAS_ONE)) * inverse(root)
            rowacc[at_rows, :] = peaks

    advance(0, 3)
    net.arrived(("rk",))
    rp_b[...] = jnp.maximum(rp_a[...], rp_dst[0])
    for j, d in enumerate(ring):
        net.start(("rx", d), rp_b, rp_dst.at[1 + j], to_x(d))
    for d in ring:
        net.arrived(("cy", d))
    cp_b[...] = jnp.maximum(
        jnp.maximum(cp_a[...], cp_dst[0]), jnp.maximum(cp_dst[1], cp_dst[2])
    )
    for d in (4, 3, 5, 2, 6, 1, 7):
        net.start(("cz", d), cp_b, cp_dst.at[2 + d], to_z(d))
    advance(3, ROWS // TILE)
    first_peaks[...] = rowacc[...].T[:BLOCKS, :]
    peaks = rp_b[...]
    for j, d in enumerate(ring):
        net.arrived(("rx", d))
        peaks = jnp.maximum(peaks, rp_dst[1 + j])
    rp_out[...] = peaks
    rinv_out[...] = jnp.broadcast_to((1.0 / peaks)[0:1, :], (LANES, ROWS)).T
    tops = cp_b[...]
    for d in range(1, NZ):
        net.arrived(("cz", d))
        tops = jnp.maximum(tops, cp_dst[2 + d])
    cp_out[...] = tops
    net.finish()


def inverse(value):
    guess = pltpu.reciprocal(value, approx=True)
    return guess * (2.0 - value * guess)


def finish_kernel(
    update_in,
    first_in,
    peaks_in,
    second,
    rinv,
    rp,
    cp,
    update,
    first_normed,
    first_peaks,
    second_normed,
    row_peaks,
    col_peaks,
    normed,
    sems,
):
    copies = [
        pltpu.make_async_copy(update_in, update, sems.at[0]),
        pltpu.make_async_copy(first_in, first_normed, sems.at[1]),
        pltpu.make_async_copy(peaks_in, first_peaks, sems.at[2]),
    ]
    for copy in copies:
        copy.start()
    row_peaks[...] = rp[0:1, :].reshape(ROWS)
    for b in range(BLOCKS):
        col_peaks[pl.ds(b * LANES, LANES)] = cp[b : b + 1, :].reshape(LANES)
    cinv = 1.0 / cp[...]
    for i in range(ROWS // FINISH):
        at_rows = pl.ds(i * FINISH, FINISH)
        for b in range(BLOCKS):
            normed[at_rows, pl.ds(b * LANES, LANES)] = (
                second[b, at_rows, :] * jnp.maximum(rinv[at_rows, :], cinv[b : b + 1, :])
            ).astype(jnp.bfloat16)
        copy = pltpu.make_async_copy(
            normed.at[at_rows], second_normed.at[at_rows], sems.at[3 + i]
        )
        copy.start()
        copies.append(copy)
    for copy in copies:
        copy.wait()


def local(activations, output_grads, first_codes, second_codes, first_scales, second_rows, second_cols):
    f32, bf16 = jnp.float32, jnp.bfloat16
    vmem = pl.BlockSpec(memory_space=pltpu.VMEM)
    hbm = pl.BlockSpec(memory_space=pltpu.HBM)
    update, first_normed, first_peaks, second, rinv, rp, cp = pl.pallas_call(
        step_kernel,
        out_shape=(
            jax.ShapeDtypeStruct((ROWS, COLS), f32),
            jax.ShapeDtypeStruct((ROWS, COLS), bf16),
            jax.ShapeDtypeStruct((BLOCKS, ROWS), f32),
            jax.ShapeDtypeStruct((BLOCKS, ROWS, LANES), f32),
            jax.ShapeDtypeStruct((ROWS, LANES), f32),
            jax.ShapeDtypeStruct((8, ROWS), f32),
            jax.ShapeDtypeStruct((BLOCKS, LANES), f32),
        ),
        in_specs=[hbm] * 7,
        out_specs=(vmem,) * 7,
        scratch_shapes=[
            pltpu.VMEM((ROWS, ROWS), bf16),
            pltpu.VMEM((ROWS, COLS // 2), jnp.int32),
            pltpu.VMEM((ROWS, COLS // 2), jnp.int32),
            pltpu.VMEM((BLOCKS, ROWS), f32),
            pltpu.VMEM((ROWS,), f32),
            pltpu.VMEM((COLS,), f32),
            pltpu.VMEM((NY * ROWS, TOKENS), bf16),
            pltpu.VMEM((CHUNKS, TOKENS, WIDTH), bf16),
            pltpu.VMEM((CHUNKS, 3, ROWS, LANES), jnp.int16),
            pltpu.VMEM((CHUNKS, 3, 8, LANES), f32),
            pltpu.VMEM((BLOCKS, ROWS, LANES), jnp.int16),
            pltpu.VMEM((BLOCKS, 8, LANES), f32),
            pltpu.VMEM((BLOCKS, ROWS, LANES), f32),
            pltpu.VMEM((8, WIDTH), f32),
            pltpu.VMEM((4, 8, LANES), f32),
            pltpu.VMEM((14, 8, LANES), f32),
            pltpu.VMEM((BLOCKS, LANES), f32),
            pltpu.VMEM((BLOCKS, LANES), f32),
            pltpu.VMEM((10, BLOCKS, LANES), f32),
            pltpu.VMEM((8, ROWS), f32),
            pltpu.VMEM((8, ROWS), f32),
            pltpu.VMEM((4, 8, ROWS), f32),
            pltpu.VMEM((ROWS, LANES), f32),
            pltpu.VMEM((BLOCKS, 8, LANES), f32),
            pltpu.SemaphoreType.DMA((n_copies(),)),
            pltpu.SemaphoreType.DMA((n_copies(),)),
            pltpu.SemaphoreType.DMA((6 + CHUNKS,)),
        ],
        compiler_params=pltpu.CompilerParams(
            collective_id=0, has_side_effects=True, vmem_limit_bytes=40 * 2**20
        ),
        name="step",
    )(
        *(
            pltpu.with_memory_space_constraint(array, pltpu.HBM)
            for array in (
                activations,
                output_grads,
                first_codes,
                second_codes,
                first_scales.T,
                second_rows,
                second_cols,
            )
        )
    )
    update, first_normed, first_peaks, second_normed, row_peaks, col_peaks = pl.pallas_call(
        finish_kernel,
        out_shape=(
            jax.ShapeDtypeStruct((ROWS, COLS), f32),
            jax.ShapeDtypeStruct((ROWS, COLS), bf16),
            jax.ShapeDtypeStruct((BLOCKS, ROWS), f32),
            jax.ShapeDtypeStruct((ROWS, COLS), bf16),
            jax.ShapeDtypeStruct((ROWS,), f32),
            jax.ShapeDtypeStruct((COLS,), f32),
        ),
        in_specs=[vmem] * 7,
        out_specs=(hbm, hbm, hbm, hbm, vmem, vmem),
        scratch_shapes=[
            pltpu.VMEM((ROWS, COLS), bf16),
            pltpu.SemaphoreType.DMA((3 + ROWS // FINISH,)),
        ],
        compiler_params=pltpu.CompilerParams(vmem_limit_bytes=16 * 2**20),
        name="finish",
    )(update, first_normed, first_peaks, second, rinv, rp, cp)
    return update, first_normed, first_peaks.T, second_normed, row_peaks, col_peaks


def solution(mesh):
    return jax.shard_map(
        local,
        mesh=mesh,
        in_specs=(
            P("col", "row"),
            P("row", "col"),
            P("row", "col"),
            P("row", "col"),
            P("row", "col"),
            P("row"),
            P("col"),
        ),
        out_specs=(
            P("row", "col"),
            P("row", "col"),
            P("row", "col"),
            P("row", "col"),
            P("row"),
            P("col"),
        ),
        check_vma=False,
    )
```

time: 115 us -> 85.7 us (0.75)
  Pallas kernels: 108 us -> 85 us
  local copies, waits for them, and re-layouts: 6.21 us -> 0 us
    pallas_call x2, Pallas kernels: 108 us -> 85 us  [the longest x1 81.6 us: local(): pl.pallas_call(step_kernel, out_shape=(jax.ShapeDtypeStruct((ROWS, COLS),...]
    unnamed x13 -> x0, local copies, waits for them, and re-layouts: 5.53 us -> none
where the time goes in v2:
time: 85.7 us; the launch traced here: 85.6 us
  Pallas kernels  85 us (99%)
    pallas_call x1, Pallas kernels, local(): pl.pallas_call(step_kernel, out_shape=(jax.ShapeDtypeStruct((ROWS, COLS),...  81.6 us
    pallas_call x1, Pallas kernels, local(): pl.pallas_call(finish_kernel, out_shape=(jax.ShapeDtypeStruct((ROWS, COLS...  3.33 us

profile of v2, /device:TPU:2, one launch (start us, length us, event | category | flops | bytes accessed | tf_op | source)
XLA Modules:
  0.0 85.6 jit_solution(10710524962630640728)
XLA Ops:
  0.6 81.6 %step.1 = (f32[256,3072]{1,0:T(8,128)S(1)}, bf16[256,3072]{1,0:T(8,128)(2,1)S(1)}, f32[24,256]{1,0:T(8,128)S(1)}, f32[24,256,128]{2,1,0:T(8,128)S(1)}, f32[256,1...) custom-call(bf16[256,256]{1,0:T(8,128)(2,1)} %act_hbm.1, bf16[64,3072]{1,0:T(8,128)(2,1)} %grads.1, ...), custom_call_target="tpu_custom_call" | custom-call | tf_op jit(solution)/shard_map/step/pallas_call | solution.py:463
  82.3 3.3 %finish.1 = (f32[256,3072]{1,0:T(8,128)}, bf16[256,3072]{1,0:T(8,128)(2,1)}, f32[24,256]{1,0:T(8,128)}, bf16[256,3072]{1,0:T(8,128)(2,1)}, f32[256]{0:T(256)}, /*index=5*/f32[3072]{0:T(1024)}) custom-call(f32[256,3072]{1,0:T(8,128)S(1)} %get-tuple-element.19.update_in, bf16[256,3072]{1,0:T(8,128)(2,1)S(1)} %get-tuple-element.20.first_in, ...), custom_call_target="tpu_custom_call" | custom-call | tf_op jit(solution)/shard_map/finish/pallas_call | solution.py:523

commit v3 on v2

--- a/solution.py
+++ b/solution.py
@@ -13,13 +13,17 @@
 COLS = 3072
 NZ, NY, NX = 8, 4, 4
 PART = COLS // NY
-CHUNKS = 6
+CHUNKS = 2
 WIDTH = PART // CHUNKS
 LANES = 128
+WB = WIDTH // LANES
 TILE = 32
 FINISH = 64
 BLOCKS = COLS // LANES
 ZROWS = TOKENS // NZ
+FAR = TOKENS - ZROWS
+PIECES = ((0, 96), (96, 80), (176, 80))
+HALF_PIECES = ((0, 48), (48, 48), (96, 32))
 TOK = TOKENS // (NZ * NY)
 
 BIAS_ONE = 1.0 - 0.9**10
@@ -53,7 +57,7 @@
 
 
 def n_copies():
-    return CHUNKS * (3 + 8 + 3 + 3) + 6 + 24 + 4 + 14 + 10 + 4
+    return CHUNKS * (3 + 24 + 3 + 3) + 6 + 24 + 4 + 17 + 10 + 7
 
 
 def step_kernel(
@@ -84,6 +88,7 @@
     gi,
     gi_scale,
     mom,
+    acc,
     sq,
     ss_src,
     ss_dst,
@@ -91,7 +96,6 @@
     cp_b,
     cp_dst,
     rp_a,
-    rp_b,
     rp_dst,
     rowacc,
     colacc,
@@ -113,13 +117,15 @@
         return (r, (x + d) % NX * 2 + k)
 
     peer = (r, x * 2 + 1 - k)
+    near = [(d, to_x(d)) for d in (1, 3, 2)] + [
+        (4 + d, (r, (x + d) % NX * 2 + 1 - k)) for d in (0, 1, 3, 2)
+    ]
 
     barrier = pltpu.get_barrier_semaphore()
     partners = (
         [to_z(d) for d in range(1, NZ)]
         + [to_y(d) for d in (1, 3, 2)]
-        + [to_x(d) for d in (1, 3, 2)]
-        + [peer]
+        + [device for _, device in near]
     )
     for partner in partners:
         pl.semaphore_signal(barrier, inc=1, device_id=partner, device_id_type=MESH)
@@ -136,20 +142,26 @@
     for load in loads:
         load.start()
 
+    def place(way, distance):
+        if distance == 4:
+            return FAR
+        return (distance if way < 0 or distance == 0 else 3 + distance) * ZROWS
+
+    def tokens(cc):
+        ahead = (cc - z + NZ) % NZ
+        return pl.ds((ahead + ahead // 4 * (11 - 2 * ahead)) * ROWS, ROWS)
+
     def spot(yy, cc, half=None):
         if half is None:
-            return at.at[pl.ds(yy * ROWS, ROWS), pl.ds(cc * ROWS, ROWS)]
+            return at.at[pl.ds(yy * ROWS, ROWS), tokens(cc)]
         size = ROWS // 2
-        return at.at[pl.ds(yy * ROWS + half * size, size), pl.ds(cc * ROWS, ROWS)]
-
-    def b_part(n, zz):
-        return bb.at[n, pl.ds(zz * ZROWS, ZROWS)]
+        return at.at[pl.ds(yy * ROWS + half * size, size), tokens(cc)]
 
     owns = []
     for n in range(CHUNKS):
         own = pltpu.make_async_copy(
             grads.at[:, pl.ds(y * PART + n * WIDTH, WIDTH)],
-            bb.at[n, pl.ds(z * ZROWS + y * TOK, TOK)],
+            bb.at[n, pl.ds(y * TOK, TOK)],
             local.at[len(pairs) + n],
         )
         own.start()
@@ -189,7 +201,6 @@
                 code = word & 15 if b % 2 == 0 else word >> 4
                 mom[b, at_rows, :] = scale[:, b : b + 1] * (code.astype(jnp.float32) - 7.5)
 
-    decode_second()
     pl.semaphore_wait(barrier, len(partners))
 
     net = Copies(send, recv)
@@ -201,7 +212,7 @@
             net.start(
                 ("b1", n, d),
                 grads.at[:, pl.ds(other * PART + n * WIDTH, WIDTH)],
-                bb.at[n, pl.ds(z * ZROWS + y * TOK, TOK)],
+                bb.at[n, pl.ds(y * TOK, TOK)],
                 to_y(d),
             )
 
@@ -210,16 +221,25 @@
             owns[n].wait()
             for d in ring:
                 net.arrived(("b1", n, d))
-        for way in (1, -1):
-            if s > 1:
-                net.arrived(("b2", n, s - 1, way))
-            zz = (z - way * (s - 1) + NZ) % NZ
-            if s < 4:
-                ref = b_part(n, zz)
-            else:
-                half = ZROWS // 2
-                ref = bb.at[n, pl.ds(zz * ZROWS + (half if way < 0 else 0), half)]
-            net.start(("b2", n, s, way), ref, ref, to_z(way))
+        for i in range(3):
+            for way in (1, -1):
+                if s > 1:
+                    net.arrived(("b2", n, s - 1, way, i))
+                for j in range(3):
+                    if s < 4:
+                        need, (first, size) = j, PIECES[j]
+                    elif way > 0:
+                        need, (first, size) = (0, 0, 1)[j], HALF_PIECES[j]
+                    else:
+                        need, (first, size) = (1, 2, 2)[j], HALF_PIECES[j]
+                        first += ZROWS // 2
+                    if need == i:
+                        net.start(
+                            ("b2", n, s, way, j),
+                            bb.at[n, pl.ds(place(way, s - 1) + first, size)],
+                            bb.at[n, pl.ds(place(way, s) + first, size)],
+                            to_z(way),
+                        )
 
     spread(0)
     for d in ring:
@@ -230,13 +250,9 @@
     for d in ring:
         ref = spot(y, c, 0)
         net.start(("axy", 0, d), ref, ref, to_x(d))
-    spread(1)
-    for d in ring:
         ref = spot(y, c, 1)
         net.start(("ayx", 0, d), ref, ref, to_y(d))
-    for n in range(2, CHUNKS):
-        spread(n)
-    decode_first()
+    decode_second()
     pass_on(0, 1)
     for e in ring:
         net.arrived(("ay", 0, e))
@@ -247,6 +263,7 @@
         ref = spot(y, (x + NX - e) % NX * 2 + k, 1)
         for d in ring:
             net.start(("ayx", e, d), ref, ref, to_y(d))
+    spread(1)
 
     def to_peer(q):
         if q == 0:
@@ -257,76 +274,90 @@
                 net.arrived(("axy", e, q))
             for d in ring:
                 net.arrived(("ayx", q, d))
-        ref = at.at[:, pl.ds(((x + NX - q) % NX * 2 + k) * ROWS, ROWS)]
+        ref = at.at[:, tokens((x + NX - q) % NX * 2 + k)]
         net.start(("peer", q), ref, ref, peer)
 
     sq[...] = jnp.zeros_like(sq)
 
-    def multiply(n):
-        for d in (2, 1, 3, 0):
-            other = (y + d) % NY
-            res = jnp.dot(
-                at[pl.ds(pl.multiple_of(other * ROWS, ROWS), ROWS), :],
-                bb[n],
-                preferred_element_type=jnp.float32,
-            )
-            tiles = res.reshape(ROWS // 8, 8, WIDTH)
-            sq[...] += jnp.sum(tiles * tiles, axis=0)
-            top = jnp.max(jnp.max(jnp.abs(tiles), axis=0), axis=0, keepdims=True)
-            top = jnp.maximum(top, 1e-30)
-            words = jnp.round(res * (32767.0 / top)).astype(jnp.int32).astype(jnp.int16)
-            scale = jnp.broadcast_to(top * (1.0 / 32767.0), (8, LANES))
-            block = y * (PART // LANES) + n
+    order = (2, 1, 3, 0)
+
+    def product(n, d, first, size):
+        other = (y + d) % NY
+        return jnp.dot(
+            at[pl.ds(pl.multiple_of(other * ROWS, ROWS), ROWS), pl.ds(first, size)],
+            bb[n, pl.ds(first, size)],
+            preferred_element_type=jnp.float32,
+        )
+
+    def pack(n, d, res):
+        tiles = res.reshape(ROWS // 8, 8, WIDTH)
+        sq[...] += jnp.sum(tiles * tiles, axis=0)
+        top = jnp.max(jnp.max(jnp.abs(tiles), axis=0), axis=0, keepdims=True)
+        top = jnp.maximum(top, 1e-30)
+        words = jnp.round(res * (32767.0 / top)).astype(jnp.int32).astype(jnp.int16)
+        scale = jnp.broadcast_to(top * (1.0 / 32767.0), (8, WIDTH))
+        block = y * (PART // LANES) + n * WB
+        for w in range(WB):
+            at_cols = slice(w * LANES, (w + 1) * LANES)
             if d:
-                gs[n, d - 1] = words
-                gs_scale[n, d - 1] = scale
-                net.start(("out", n, d), gs.at[n, d - 1], gi.at[block], to_y(d))
-                net.start(("scale", n, d), gs_scale.at[n, d - 1], gi_scale.at[block], to_y(d))
+                gs[n, d - 1, w] = words[:, at_cols]
+                gs_scale[n, d - 1, w] = scale[:, at_cols]
             else:
-                gi[block] = words
-                gi_scale[block] = scale
-
-    extra = {
-        4: [lambda: to_peer(0)],
-        5: [lambda: to_peer(1), lambda: to_peer(3), lambda: to_peer(2)],
-    }
-    done = 0
-    for slot in range(2, CHUNKS + 5):
-        for n in range(CHUNKS):
-            s = slot - n
-            if 1 <= s <= 4 and (n, s) != (0, 1):
-                pass_on(n, s)
-        for step in extra.get(slot, ()):
-            step()
-        if slot >= 6 or slot == CHUNKS + 4:
-            last = slot == CHUNKS + 4
-            upto = CHUNKS if last else slot - 5
-            if done == 0:
-                for q in (0,) + ring:
-                    net.arrived(("peer", q))
-            while done < upto:
-                for way in (1, -1):
-                    net.arrived(("b2", done, 4, way))
-                multiply(done)
-                done += 1
+                gi[block + w] = words[:, at_cols]
+                gi_scale[block + w] = scale[:, at_cols]
+
+    def hand_out(n, d):
+        block = pl.ds(y * (PART // LANES) + n * WB, WB)
+        net.start(("out", n, d), gs.at[n, d - 1], gi.at[block], to_y(d))
+        net.start(("scale", n, d), gs_scale.at[n, d - 1], gi_scale.at[block], to_y(d))
+
+    def far_arrived(n):
+        for way in (1, -1):
+            for j in range(3):
+                net.arrived(("b2", n, 4, way, j))
+
+    pass_on(0, 2)
+    decode_first()
+    pass_on(0, 3)
+    pass_on(1, 1)
+    pass_on(0, 4)
+    pass_on(1, 2)
+    for q in (0,) + ring:
+        to_peer(q)
+    pass_on(1, 3)
+    for q in (0,) + ring:
+        net.arrived(("peer", q))
+    far_arrived(0)
+    for d in order:
+        pack(0, d, product(0, d, 0, TOKENS))
+        if d:
+            hand_out(0, d)
+    pass_on(1, 4)
+    for d in order:
+        acc[d] = product(1, d, 0, FAR)
+    far_arrived(1)
+    for d in order:
+        pack(1, d, acc[d] + product(1, d, FAR, ZROWS))
 
     ss_src[0] = jnp.full((8, LANES), jnp.sum(sq[...]))
+    stages = [
+        near,
+        [(d, to_z(d)) for d in (4, 3, 5, 2, 6, 1, 7)],
+        [(d, to_y(d)) for d in ring],
+    ]
     slot = 0
-    stages = [
-        [(0, peer)],
-        [(d, to_x(d)) for d in ring],
-        [(d, to_y(d)) for d in ring],
-        [(d, to_z(d)) for d in range(1, NZ)],
-    ]
     for i, stage in enumerate(stages):
         for j, (d, device) in enumerate(stage):
             net.start(("ss", i, d), ss_src.at[i], ss_dst.at[slot + j], device)
+        if i == 0:
+            for d in ring:
+                hand_out(1, d)
         total = ss_src[i]
         for j, (d, device) in enumerate(stage):
             net.arrived(("ss", i, d))
             total = total + ss_dst[slot + j]
         slot += len(stage)
-        if i < 3:
+        if i < 2:
             ss_src[i + 1] = total
     limit = float(D) * FF
     clip = jnp.where(total <= limit, 1.0, jnp.sqrt(limit / jnp.maximum(total, limit)))
@@ -358,7 +389,8 @@
     for j, d in enumerate(ring):
         net.start(("cy", d), cp_a, cp_dst.at[j], to_y(d))
     rp_a[...] = jnp.broadcast_to(jnp.max(rowacc[...].T, axis=0, keepdims=True), (8, ROWS))
-    net.start(("rk",), rp_a, rp_dst.at[0], peer)
+    for j, (d, device) in enumerate(near):
+        net.start(("rx", d), rp_a, rp_dst.at[j], device)
 
     def advance(first, last):
         lane = lax.broadcasted_iota(jnp.int32, (TILE, LANES), 1)
@@ -381,10 +413,6 @@
             rowacc[at_rows, :] = peaks
 
     advance(0, 3)
-    net.arrived(("rk",))
-    rp_b[...] = jnp.maximum(rp_a[...], rp_dst[0])
-    for j, d in enumerate(ring):
-        net.start(("rx", d), rp_b, rp_dst.at[1 + j], to_x(d))
     for d in ring:
         net.arrived(("cy", d))
     cp_b[...] = jnp.maximum(
@@ -394,10 +422,10 @@
         net.start(("cz", d), cp_b, cp_dst.at[2 + d], to_z(d))
     advance(3, ROWS // TILE)
     first_peaks[...] = rowacc[...].T[:BLOCKS, :]
-    peaks = rp_b[...]
-    for j, d in enumerate(ring):
+    peaks = rp_a[...]
+    for j, (d, _) in enumerate(near):
         net.arrived(("rx", d))
-        peaks = jnp.maximum(peaks, rp_dst[1 + j])
+        peaks = jnp.maximum(peaks, rp_dst[j])
     rp_out[...] = peaks
     rinv_out[...] = jnp.broadcast_to((1.0 / peaks)[0:1, :], (LANES, ROWS)).T
     tops = cp_b[...]
@@ -482,20 +510,20 @@
             pltpu.VMEM((COLS,), f32),
             pltpu.VMEM((NY * ROWS, TOKENS), bf16),
             pltpu.VMEM((CHUNKS, TOKENS, WIDTH), bf16),
-            pltpu.VMEM((CHUNKS, 3, ROWS, LANES), jnp.int16),
-            pltpu.VMEM((CHUNKS, 3, 8, LANES), f32),
+            pltpu.VMEM((CHUNKS, 3, WB, ROWS, LANES), jnp.int16),
+            pltpu.VMEM((CHUNKS, 3, WB, 8, LANES), f32),
             pltpu.VMEM((BLOCKS, ROWS, LANES), jnp.int16),
             pltpu.VMEM((BLOCKS, 8, LANES), f32),
             pltpu.VMEM((BLOCKS, ROWS, LANES), f32),
+            pltpu.VMEM((NY, ROWS, WIDTH), f32),
             pltpu.VMEM((8, WIDTH), f32),
-            pltpu.VMEM((4, 8, LANES), f32),
-            pltpu.VMEM((14, 8, LANES), f32),
+            pltpu.VMEM((3, 8, LANES), f32),
+            pltpu.VMEM((17, 8, LANES), f32),
             pltpu.VMEM((BLOCKS, LANES), f32),
             pltpu.VMEM((BLOCKS, LANES), f32),
             pltpu.VMEM((10, BLOCKS, LANES), f32),
             pltpu.VMEM((8, ROWS), f32),
-            pltpu.VMEM((8, ROWS), f32),
-            pltpu.VMEM((4, 8, ROWS), f32),
+            pltpu.VMEM((7, 8, ROWS), f32),
             pltpu.VMEM((ROWS, LANES), f32),
             pltpu.VMEM((BLOCKS, 8, LANES), f32),
             pltpu.SemaphoreType.DMA((n_copies(),)),

time: 85.7 us -> 79.1 us (0.923)
  Pallas kernels: 85 us -> 78.3 us
    pallas_call x1, Pallas kernels: 81.6 us -> 75 us  [local(): pl.pallas_call(step_kernel, out_shape=(jax.ShapeDtypeStruct((ROWS, COLS),...]
where the time goes in v3:
time: 79.1 us; the launch traced here: 79 us
  Pallas kernels  78.3 us (99%)
    pallas_call x1, Pallas kernels, local(): pl.pallas_call(step_kernel, out_shape=(jax.ShapeDtypeStruct((ROWS, COLS),...  75 us
    pallas_call x1, Pallas kernels, local(): pl.pallas_call(finish_kernel, out_shape=(jax.ShapeDtypeStruct((ROWS, COLS...  3.33 us

profile of v3, /device:TPU:2, one launch (start us, length us, event | category | flops | bytes accessed | tf_op | source)
XLA Modules:
  0.0 79.0 jit_solution(868564369465443378)
XLA Ops:
  0.6 75.0 %step.1 = (f32[256,3072]{1,0:T(8,128)S(1)}, bf16[256,3072]{1,0:T(8,128)(2,1)S(1)}, f32[24,256]{1,0:T(8,128)S(1)}, f32[24,256,128]{2,1,0:T(8,128)S(1)}, f32[256,1...) custom-call(bf16[256,256]{1,0:T(8,128)(2,1)} %act_hbm.1, bf16[64,3072]{1,0:T(8,128)(2,1)} %grads.1, ...), custom_call_target="tpu_custom_call" | custom-call | tf_op jit(solution)/shard_map/step/pallas_call | solution.py:491
  75.6 3.3 %finish.1 = (f32[256,3072]{1,0:T(8,128)}, bf16[256,3072]{1,0:T(8,128)(2,1)}, f32[24,256]{1,0:T(8,128)}, bf16[256,3072]{1,0:T(8,128)(2,1)}, f32[256]{0:T(256)}, /*index=5*/f32[3072]{0:T(1024)}) custom-call(f32[256,3072]{1,0:T(8,128)S(1)} %get-tuple-element.19.update_in, bf16[256,3072]{1,0:T(8,128)(2,1)S(1)} %get-tuple-element.20.first_in, ...), custom_call_target="tpu_custom_call" | custom-call | tf_op jit(solution)/shard_map/finish/pallas_call | solution.py:551

commit v4 on v3

--- a/solution.py
+++ b/solution.py
@@ -22,8 +22,7 @@
 BLOCKS = COLS // LANES
 ZROWS = TOKENS // NZ
 FAR = TOKENS - ZROWS
-PIECES = ((0, 96), (96, 80), (176, 80))
-HALF_PIECES = ((0, 48), (48, 48), (96, 32))
+SPLIT = (192, 64)
 TOK = TOKENS // (NZ * NY)
 
 BIAS_ONE = 1.0 - 0.9**10
@@ -57,7 +56,7 @@
 
 
 def n_copies():
-    return CHUNKS * (3 + 24 + 3 + 3) + 6 + 24 + 4 + 17 + 10 + 7
+    return CHUNKS * (3 + 28 + 3 + 3) + 6 + 24 + 4 + 17 + 10 + 7
 
 
 def step_kernel(
@@ -123,7 +122,7 @@
 
     barrier = pltpu.get_barrier_semaphore()
     partners = (
-        [to_z(d) for d in range(1, NZ)]
+        [to_z(d) for d in (1, 7)]
         + [to_y(d) for d in (1, 3, 2)]
         + [device for _, device in near]
     )
@@ -154,8 +153,7 @@
     def spot(yy, cc, half=None):
         if half is None:
             return at.at[pl.ds(yy * ROWS, ROWS), tokens(cc)]
-        size = ROWS // 2
-        return at.at[pl.ds(yy * ROWS + half * size, size), tokens(cc)]
+        return at.at[pl.ds(yy * ROWS + half * SPLIT[0], SPLIT[half]), tokens(cc)]
 
     owns = []
     for n in range(CHUNKS):
@@ -216,31 +214,26 @@
                 to_y(d),
             )
 
-    def pass_on(n, s):
-        if s == 1:
-            owns[n].wait()
-            for d in ring:
+    def pass_on(n, s, pieces=(0, 1, 2, 3)):
+        for i in pieces:
+            d = ((0,) + ring)[i]
+            if s == 1 and d:
                 net.arrived(("b1", n, d))
-        for i in range(3):
+            elif s == 1:
+                owns[n].wait()
+            first = (y - d + NY) % NY * TOK
             for way in (1, -1):
                 if s > 1:
                     net.arrived(("b2", n, s - 1, way, i))
-                for j in range(3):
-                    if s < 4:
-                        need, (first, size) = j, PIECES[j]
-                    elif way > 0:
-                        need, (first, size) = (0, 0, 1)[j], HALF_PIECES[j]
-                    else:
-                        need, (first, size) = (1, 2, 2)[j], HALF_PIECES[j]
-                        first += ZROWS // 2
-                    if need == i:
-                        net.start(
-                            ("b2", n, s, way, j),
-                            bb.at[n, pl.ds(place(way, s - 1) + first, size)],
-                            bb.at[n, pl.ds(place(way, s) + first, size)],
-                            to_z(way),
-                        )
-
+                if s < 4 or (way > 0) == (i < 2):
+                    net.start(
+                        ("b2", n, s, way, i),
+                        bb.at[n, pl.ds(place(way, s - 1) + first, TOK)],
+                        bb.at[n, pl.ds(place(way, s) + first, TOK)],
+                        to_z(way),
+                    )
+
+    pass_on(0, 1, (0,))
     spread(0)
     for d in ring:
         ref = spot(y, c, 0)
@@ -252,8 +245,7 @@
         net.start(("axy", 0, d), ref, ref, to_x(d))
         ref = spot(y, c, 1)
         net.start(("ayx", 0, d), ref, ref, to_y(d))
-    decode_second()
-    pass_on(0, 1)
+    pass_on(0, 1, (1, 2, 3))
     for e in ring:
         net.arrived(("ay", 0, e))
         ref = spot((y + NY - e) % NY, c, 0)
@@ -312,14 +304,14 @@
         net.start(("scale", n, d), gs_scale.at[n, d - 1], gi_scale.at[block], to_y(d))
 
     def far_arrived(n):
-        for way in (1, -1):
-            for j in range(3):
-                net.arrived(("b2", n, 4, way, j))
+        for i in range(NY):
+            net.arrived(("b2", n, 4, 1 if i < 2 else -1, i))
 
     pass_on(0, 2)
-    decode_first()
+    decode_second()
     pass_on(0, 3)
     pass_on(1, 1)
+    decode_first()
     pass_on(0, 4)
     pass_on(1, 2)
     for q in (0,) + ring:

time: 79.1 us -> 75.4 us (0.953)
  Pallas kernels: 78.3 us -> 74.7 us
    pallas_call x1, Pallas kernels: 75 us -> 71.4 us  [local(): pl.pallas_call(step_kernel, out_shape=(jax.ShapeDtypeStruct((ROWS, COLS),...]
where the time goes in v4:
time: 75.4 us; the launch traced here: 75.3 us
  Pallas kernels  74.7 us (99%)
    pallas_call x1, Pallas kernels, local(): pl.pallas_call(step_kernel, out_shape=(jax.ShapeDtypeStruct((ROWS, COLS),...  71.4 us
    pallas_call x1, Pallas kernels, local(): pl.pallas_call(finish_kernel, out_shape=(jax.ShapeDtypeStruct((ROWS, COLS...  3.33 us

profile of v4, /device:TPU:2, one launch (start us, length us, event | category | flops | bytes accessed | tf_op | source)
XLA Modules:
  0.0 75.3 jit_solution(8479798591286868547)
XLA Ops:
  0.6 71.4 %step.1 = (f32[256,3072]{1,0:T(8,128)S(1)}, bf16[256,3072]{1,0:T(8,128)(2,1)S(1)}, f32[24,256]{1,0:T(8,128)S(1)}, f32[24,256,128]{2,1,0:T(8,128)S(1)}, f32[256,1...) custom-call(bf16[256,256]{1,0:T(8,128)(2,1)} %act_hbm.1, bf16[64,3072]{1,0:T(8,128)(2,1)} %grads.1, ...), custom_call_target="tpu_custom_call" | custom-call | tf_op jit(solution)/shard_map/step/pallas_call | solution.py:483
  72.0 3.3 %finish.1 = (f32[256,3072]{1,0:T(8,128)}, bf16[256,3072]{1,0:T(8,128)(2,1)}, f32[24,256]{1,0:T(8,128)}, bf16[256,3072]{1,0:T(8,128)(2,1)}, f32[256]{0:T(256)}, /*index=5*/f32[3072]{0:T(1024)}) custom-call(f32[256,3072]{1,0:T(8,128)S(1)} %get-tuple-element.19.update_in, bf16[256,3072]{1,0:T(8,128)(2,1)S(1)} %get-tuple-element.20.first_in, ...), custom_call_target="tpu_custom_call" | custom-call | tf_op jit(solution)/shard_map/finish/pallas_call | solution.py:543

commit v5 on v4

--- a/solution.py
+++ b/solution.py
@@ -124,7 +124,7 @@
     partners = (
         [to_z(d) for d in (1, 7)]
         + [to_y(d) for d in (1, 3, 2)]
-        + [device for _, device in near]
+        + [device for d, device in near if d <= 4]
     )
     for partner in partners:
         pl.semaphore_signal(barrier, inc=1, device_id=partner, device_id_type=MESH)
@@ -246,7 +246,8 @@
         ref = spot(y, c, 1)
         net.start(("ayx", 0, d), ref, ref, to_y(d))
     pass_on(0, 1, (1, 2, 3))
-    for e in ring:
+
+    def relay(e):
         net.arrived(("ay", 0, e))
         ref = spot((y + NY - e) % NY, c, 0)
         for d in ring:
@@ -255,6 +256,11 @@
         ref = spot(y, (x + NX - e) % NX * 2 + k, 1)
         for d in ring:
             net.start(("ayx", e, d), ref, ref, to_y(d))
+
+    relay(1)
+    pass_on(0, 2)
+    relay(3)
+    relay(2)
     spread(1)
 
     def to_peer(q):
@@ -307,7 +313,6 @@
         for i in range(NY):
             net.arrived(("b2", n, 4, 1 if i < 2 else -1, i))
 
-    pass_on(0, 2)
     decode_second()
     pass_on(0, 3)
     pass_on(1, 1)
@@ -360,6 +365,7 @@
             net.arrived(("scale", n, d))
 
     rate = clip[0:1, :]
+    tenth = 0.1 * rate
     colacc[...] = jnp.zeros_like(colacc)
 
     @pl.loop(0, ROWS // TILE)
@@ -371,7 +377,6 @@
             scaled = words * (gi_scale[b, 0:1, :] * rate)
             value = second[b, at_rows, :] + 0.05 * scaled * scaled
             second[b, at_rows, :] = value
-            mom[b, at_rows, :] += 0.1 * scaled
             best = jnp.maximum(best, value)
             colacc[b] = jnp.maximum(colacc[b], jnp.max(value.reshape(TILE // 8, 8, LANES), axis=0))
         rowacc[at_rows, :] = best
@@ -393,7 +398,8 @@
             peaks = jnp.zeros((TILE, LANES), jnp.float32)
             for b in range(BLOCKS):
                 at_cols = pl.ds(b * LANES, LANES)
-                value = mom[b, at_rows, :]
+                words = gi[b, at_rows, :].astype(jnp.int32).astype(jnp.float32)
+                value = mom[b, at_rows, :] + words * (gi_scale[b, 0:1, :] * tenth)
                 peak = jnp.max(jnp.abs(value), axis=1, keepdims=True)
                 peaks = jnp.where(lane == b, peak, peaks)
                 first_normed[at_rows, at_cols] = (value * inverse(peak + 1e-06)).astype(

time: 75.4 us -> 74.5 us (0.988)
  Pallas kernels: 74.7 us -> 73.8 us
    pallas_call x1, Pallas kernels: 71.4 us -> 70.5 us  [local(): pl.pallas_call(step_kernel, out_shape=(jax.ShapeDtypeStruct((ROWS, COLS),...]
where the time goes in v5:
time: 74.5 us; the launch traced here: 74.4 us
  Pallas kernels  73.8 us (99%)
    pallas_call x1, Pallas kernels, local(): pl.pallas_call(step_kernel, out_shape=(jax.ShapeDtypeStruct((ROWS, COLS),...  70.5 us
    pallas_call x1, Pallas kernels, local(): pl.pallas_call(finish_kernel, out_shape=(jax.ShapeDtypeStruct((ROWS, COLS...  3.33 us

profile of v5, /device:TPU:2, one launch (start us, length us, event | category | flops | bytes accessed | tf_op | source)
XLA Modules:
  0.0 74.4 jit_solution(4352348816177728442)
XLA Ops:
  0.6 70.5 %step.1 = (f32[256,3072]{1,0:T(8,128)S(1)}, bf16[256,3072]{1,0:T(8,128)(2,1)S(1)}, f32[24,256]{1,0:T(8,128)S(1)}, f32[24,256,128]{2,1,0:T(8,128)S(1)}, f32[256,1...) custom-call(bf16[256,256]{1,0:T(8,128)(2,1)} %act_hbm.1, bf16[64,3072]{1,0:T(8,128)(2,1)} %grads.1, ...), custom_call_target="tpu_custom_call" | custom-call | tf_op jit(solution)/shard_map/step/pallas_call | solution.py:489
  71.1 3.3 %finish.1 = (f32[256,3072]{1,0:T(8,128)}, bf16[256,3072]{1,0:T(8,128)(2,1)}, f32[24,256]{1,0:T(8,128)}, bf16[256,3072]{1,0:T(8,128)(2,1)}, f32[256]{0:T(256)}, /*index=5*/f32[3072]{0:T(1024)}) custom-call(f32[256,3072]{1,0:T(8,128)S(1)} %get-tuple-element.19.update_in, bf16[256,3072]{1,0:T(8,128)(2,1)S(1)} %get-tuple-element.20.first_in, ...), custom_call_target="tpu_custom_call" | custom-call | tf_op jit(solution)/shard_map/finish/pallas_call | solution.py:549

commit v6 on v5

--- a/solution.py
+++ b/solution.py
@@ -164,8 +164,6 @@
         )
         own.start()
         owns.append(own)
-    loads[0].wait()
-    spot(y, c)[...] = act[...].T
 
     def decode_second():
         for load in loads[1:4]:
@@ -235,6 +233,8 @@
 
     pass_on(0, 1, (0,))
     spread(0)
+    loads[0].wait()
+    spot(y, c)[...] = act[...].T
     for d in ring:
         ref = spot(y, c, 0)
         net.start(("ay", 0, d), ref, ref, to_y(d))
@@ -454,6 +454,8 @@
     row_peaks,
     col_peaks,
     normed,
+    row_line,
+    col_line,
     sems,
 ):
     copies = [
@@ -463,9 +465,16 @@
     ]
     for copy in copies:
         copy.start()
-    row_peaks[...] = rp[0:1, :].reshape(ROWS)
+    row_line[...] = rp[0:1, :].reshape(ROWS)
     for b in range(BLOCKS):
-        col_peaks[pl.ds(b * LANES, LANES)] = cp[b : b + 1, :].reshape(LANES)
+        col_line[pl.ds(b * LANES, LANES)] = cp[b : b + 1, :].reshape(LANES)
+    lines = [
+        pltpu.make_async_copy(row_line, row_peaks, sems.at[3 + ROWS // FINISH]),
+        pltpu.make_async_copy(col_line, col_peaks, sems.at[4 + ROWS // FINISH]),
+    ]
+    for line in lines:
+        line.start()
+    copies += lines
     cinv = 1.0 / cp[...]
     for i in range(ROWS // FINISH):
         at_rows = pl.ds(i * FINISH, FINISH)
@@ -557,10 +566,12 @@
             jax.ShapeDtypeStruct((COLS,), f32),
         ),
         in_specs=[vmem] * 7,
-        out_specs=(hbm, hbm, hbm, hbm, vmem, vmem),
+        out_specs=(hbm,) * 6,
         scratch_shapes=[
             pltpu.VMEM((ROWS, COLS), bf16),
-            pltpu.SemaphoreType.DMA((3 + ROWS // FINISH,)),
+            pltpu.VMEM((ROWS,), f32),
+            pltpu.VMEM((COLS,), f32),
+            pltpu.SemaphoreType.DMA((5 + ROWS // FINISH,)),
         ],
         compiler_params=pltpu.CompilerParams(vmem_limit_bytes=16 * 2**20),
         name="finish",

time: 74.5 us -> 73.9 us (level)
  no operation moved by 1% of the time
where the time goes in v6:
time: 73.9 us
  Pallas kernels  73.2 us (99%)
    pallas_call x1, Pallas kernels, local(): pl.pallas_call(step_kernel, out_shape=(jax.ShapeDtypeStruct((ROWS, COLS),...  70.5 us
    pallas_call x1, Pallas kernels, local(): pl.pallas_call(finish_kernel, out_shape=(jax.ShapeDtypeStruct((ROWS, COLS...  2.75 us

profile of v6, /device:TPU:2, one launch (start us, length us, event | category | flops | bytes accessed | tf_op | source)
XLA Modules:
  0.0 73.9 jit_solution(10578767441240827859)
XLA Ops:
  0.6 70.5 %step.1 = (f32[256,3072]{1,0:T(8,128)S(1)}, bf16[256,3072]{1,0:T(8,128)(2,1)S(1)}, f32[24,256]{1,0:T(8,128)S(1)}, f32[24,256,128]{2,1,0:T(8,128)S(1)}, f32[256,1...) custom-call(bf16[256,256]{1,0:T(8,128)(2,1)} %act_hbm.1, bf16[64,3072]{1,0:T(8,128)(2,1)} %grads.1, ...), custom_call_target="tpu_custom_call" | custom-call | tf_op jit(solution)/shard_map/step/pallas_call | solution.py:498
  71.1 2.8 %finish.1 = (f32[256,3072]{1,0:T(8,128)}, bf16[256,3072]{1,0:T(8,128)(2,1)}, f32[24,256]{1,0:T(8,128)}, bf16[256,3072]{1,0:T(8,128)(2,1)}, f32[256]{0:T(256)}, /*index=5*/f32[3072]{0:T(1024)}) custom-call(f32[256,3072]{1,0:T(8,128)S(1)} %get-tuple-element.19.update_in, bf16[256,3072]{1,0:T(8,128)(2,1)S(1)} %get-tuple-element.20.first_in, ...), custom_call_target="tpu_custom_call" | custom-call | tf_op jit(solution)/shard_map/finish/pallas_call | solution.py:558
